TPU v7x, 32 devices: a whole 2x2x4 slice. The times are simulated.
32 devices in a mesh: dp: 8 (over y, x, core), expert: 4 (over z).
Axes of the slice: x: 2, y: 2, z: 4, core: 2. Of those that a mesh axis runs over, the one named last changes fastest.
Arguments:
- tokens: bfloat16 [4096, 3072], P(('dp', 'expert')), parts along dimension 0, may hold values from -6 to 6
- w_gate: bfloat16 [3072, 8192], P(None, 'expert'), may hold values from -0.109375 to 0.109375
- w_up: bfloat16 [3072, 8192], P(None, 'expert'), may hold values from -0.109375 to 0.109375
- w_down: bfloat16 [8192, 3072], P('expert'), may hold values from -0.0625 to 0.0625
- route_ids: int32 [4096, 2], P(('dp', 'expert')), parts along dimension 0, may hold values from 0 to 7, as said below
- route_prob: float32 [4096], P(('dp', 'expert')), parts along dimension 0, may hold values from 0.5 to 0.95
- slot_index: int32 [4096], P(('dp', 'expert')), parts along dimension 0, may hold values from 0 to 64, as said below
Outputs:
- mixed: bfloat16 [4096, 3072], P(('dp', 'expert')), parts along dimension 0
There are 8 independent parts, one for each index of `dp`. A program takes and returns all parts, laid end to end along the dimension named above; an argument that names none is the same for every part. Nothing has to cross between parts.
Inputs may be any that keep to these rules, and one draw needn't show every extreme that they name: `route_ids`: each row names two different experts. `slot_index`: a token of whose two experts one is expert 0 holds its rank, in row order, among the tokens of its device that name expert 0; every other token holds 64. At most 64 of one device's 128 tokens name expert 0, and some device has exactly 64; the router's capacity of 64 tokens for expert 0 is counted over each aligned pair of 256 tokens (blocks 2k and 2k + 1) and is always filled, so those two devices have exactly 64 such tokens together.
All inputs are finite; a program needn't handle non-finite values.
Results may differ from a plain program's by a relative error of at most 0.023.
Values may be sent and summed in bfloat16 or wider, within the bound.
A program may use at most 128 MiB of HBM per device.

v0:
```python
import jax
import jax.numpy as jnp
from jax import lax
from jax.sharding import PartitionSpec as P


def shards(tokens, w_gate, w_up, w_down, route_ids, route_prob, slot_index):
    local_count = tokens.shape[0]
    capacity = local_count // 2
    share = jnp.where(
        route_ids[:, 0] == 0, route_prob, jnp.where(route_ids[:, 1] == 0, 1.0 - route_prob, 0.0)
    )
    share = jnp.where(slot_index < capacity, share, 0.0)
    picker = slot_index[None, :] == jnp.arange(capacity, dtype=jnp.int32)[:, None]
    picker_half = picker.astype(jnp.bfloat16)
    source = jnp.dot(picker_half, tokens, preferred_element_type=jnp.float32).astype(jnp.bfloat16)
    row_share = jnp.dot(picker.astype(jnp.float32), share, precision=lax.Precision.HIGHEST)
    block = lax.all_gather(source, "expert", axis=0, tiled=True)
    gate = jnp.dot(block, w_gate, preferred_element_type=jnp.float32)
    up = jnp.dot(block, w_up, preferred_element_type=jnp.float32)
    hidden = (jax.nn.silu(gate) * up).astype(jnp.bfloat16)
    partial_value = jnp.dot(hidden, w_down, preferred_element_type=jnp.float32).astype(jnp.bfloat16)
    partial_value = lax.optimization_barrier(partial_value)
    terms = partial_value.astype(jnp.float32)
    down = lax.psum_scatter(
        terms.astype(jnp.bfloat16), "expert", scatter_dimension=0, tiled=True
    ).astype(jnp.float32)
    scaled = (row_share[:, None] * down).astype(jnp.bfloat16)
    placed = jnp.einsum("cr,cd->rd", picker_half, scaled, preferred_element_type=jnp.float32)
    return placed.astype(jnp.bfloat16)


def solution(mesh):
    return jax.shard_map(
        shards,
        mesh=mesh,
        in_specs=(
            P(("dp", "expert"), None),
            P(None, "expert"),
            P(None, "expert"),
            P("expert", None),
            P(("dp", "expert"), None),
            P(("dp", "expert")),
            P(("dp", "expert")),
        ),
        out_specs=P(("dp", "expert"), None),
        check_vma=False,
    )
```

profile of v0, /device:TPU:0, one launch (start us, length us, event | category | flops | bytes accessed | tf_op | source)
XLA Modules:
  0.0 119.6 jit_solution(8722771579992600894)
XLA Ops:
  6.5 0.0 copy-start
  6.5 0.0 all-gather.2.cloned.1.call-start
  6.5 1.1 copy-done
  7.7 1.7 %convolution_convert_fusion.2 = bf16[64,3072]{1,0:T(8,128)(2,1)} fusion(bf16[128,3072]{1,0:T(8,128)(2,1)S(1)} %copy-done, s32[128]{0:T(128)} %param.13), kind=kOutput, calls=%fused_computation.2 | convolution fusion | flops 50536448 | bytes 1180160 | tf_op jit(solution)/shard_map/dot_general | solution.py:16
  9.3 0.0 all-gather.2.cloned.1.call-update
  9.3 0.0 reduce-scatter.2.cloned.1.call-start
  9.4 39.9 %all-gather.2.cloned.1.call-done = bf16[256,3072]{1,0:T(8,128)(2,1)} async-done(((bf16[64,3072]{1,0:T(8,128)(2,1)}), bf16[256,3072]{1,0:T(8,128)(2,1)}) %all-gather.2.cloned.1.call-update) | async-done | bytes 1572880 | tf_op jit(solution)/shard_map/all_gather | solution.py:18
  49.3 0.0 copy-start.2
  49.3 9.9 %fusion.19 = f32[256,2048]{1,0:T(8,128)} fusion(bf16[256,3072]{1,0:T(8,128)(2,1)} %all-gather.2.cloned.1.call-done, bf16[3072,2048]{1,0:T(8,128)(2,1)} %param.8), kind=kOutput, calls=%fused_computation.28 | convolution fusion | flops 3221225472 | bytes 16252928 | tf_op jit(solution)/shard_map/dot_general | solution.py:19
  59.2 0.0 copy-done.2
  59.2 0.0 copy-start.1
  59.2 0.0 copy-start.3
  59.2 0.0 copy-start.4
  59.2 16.9 %convolution_convert_fusion = bf16[256,3072]{1,0:T(8,128)(2,1)} fusion(bf16[2048,3072]{1,0:T(8,128)(2,1)} %param.10, bf16[256,3072]{1,0:T(8,128)(2,1)S(1)} %copy-done.2, bf16[3072,2048]{1,0:T(8,128)(2,1)} %param.9, f32[256,2048]{1,0:T(8,128)} %fusion.19), kind=kOutput, calls=%fused_computation | convolution fusion | flops 6446383104 | bytes 30408704 | tf_op jit(solution)/shard_map/dot_general | solution.py:22
  76.2 0.0 reduce-scatter.2.cloned.1.call-update
  76.2 0.0 copy-done.1
  76.2 0.0 copy-done.3
  76.2 0.0 copy-done.4
  76.2 0.1 convolution_bitcast_fusion
  76.3 34.1 %reduce-scatter.2.cloned.1.call-done = bf16[64,3072]{1,0:T(8,128)(2,1)} async-done(((bf16[256,3072]{1,0:T(8,128)(2,1)}), bf16[64,3072]{1,0:T(8,128)(2,1)}) %reduce-scatter.2.cloned.1.call-update) | async-done | bytes 393232 | tf_op jit(solution)/shard_map/reduce_scatter | solution.py:25
  110.5 2.3 %convolution_convert_fusion.1 = bf16[128,3072]{1,0:T(8,128)(2,1)} fusion(bf16[64,3072]{1,0:T(8,128)(2,1)} %reduce-scatter.2.cloned.1.call-done, f32[64]{0:T(128)S(1)} %convolution_bitcast_fusion, s32[128]{0:T(128)S(1)} %copy-done.1), kind=kOutput, calls=%fused_computation.1 | convolution fusion | flops 51322880 | bytes 1180416 | tf_op jit(solution)/shard_map/cr,cd->rd/dot_general | solution.py:29
Async XLA Ops:
  6.5 1.1 copy-start
  6.5 42.8 %all-gather.2.cloned.1.call-start = ((), (), s32[]{:S(2)}) async-start(), calls=%async_computation.1 | async-start | bytes 1966080 | tf_op jit(solution)/shard_map/all_gather | solution.py:18
  9.3 101.1 %reduce-scatter.2.cloned.1.call-start = ((), (), s32[]{:S(2)}) async-start(), calls=%async_computation.2 | async-start | bytes 1966080 | tf_op jit(solution)/shard_map/reduce_scatter | solution.py:25
  49.3 9.9 %copy-start.2 = (bf16[256,3072]{1,0:T(8,128)(2,1)S(1)}, bf16[256,3072]{1,0:T(8,128)(2,1)}, u32[]{:S(2)}) copy-start(bf16[256,3072]{1,0:T(8,128)(2,1)} %all-gather.2.cloned.1.call-done) | copy-start | bytes 4718596
  59.2 17.0 %copy-start.1 = (s32[128]{0:T(128)S(1)}, s32[128]{0:T(128)}, u32[]{:S(2)}) copy-start(s32[128]{0:T(128)} %param.13) | copy-start | bytes 1540
  59.2 17.0 %copy-start.3 = (s32[128,2]{0,1:T(2,128)S(1)}, s32[128,2]{0,1:T(2,128)}, u32[]{:S(2)}) copy-start(s32[128,2]{0,1:T(2,128)} %param.11) | copy-start | bytes 3076
  59.2 17.0 %copy-start.4 = (f32[128]{0:T(128)S(1)}, f32[128]{0:T(128)}, u32[]{:S(2)}) copy-start(f32[128]{0:T(128)} %param.12) | copy-start | bytes 1540
Sparse Core Ops, SparseCore 0:
  9.5 39.7 all-gather.1
  76.3 34.1 reduce-scatter.1
where the time goes:
time: 120 us
  waiting for transfers between devices  74.1 us (62%)
  matrix products  30.9 us (26%)
  between operations  13.4 us (11%)
    all_gather x1, waiting for transfers between devices, shards(): block = lax.all_gather(source, 'expert', axis=0, tiled=True)  39.9 us
    reduce_scatter x1, waiting for transfers between devices, shards(): lax.psum_scatter(terms.astype(jnp.bfloat16), 'expert', scatter_dimension=...  34.1 us
    dot_general x1, matrix products, shards(): jnp.dot(hidden, w_down, preferred_element_type=jnp.float32)  16.9 us
    dot_general x1, matrix products, shards(): gate = jnp.dot(block, w_gate, preferred_element_type=jnp.float32)  9.92 us
  transfers between devices with their start and end apart: 2, of which 2 were waited for; matrix products, arithmetic and copies ran while one was open for 0% of the time, Pallas kernels for 0%

commit v1 on v0

v1 whole, which is shorter than its diff:
```python
import functools

import jax
import jax.numpy as jnp
from jax import lax
from jax.experimental import pallas as pl
from jax.experimental.pallas import tpu as pltpu
from jax.sharding import PartitionSpec as P

MESH = pl.DeviceIdType.MESH
F32 = jnp.float32
BF16 = jnp.bfloat16


def loop(lo, hi):
    def run(body):
        def step(i, carry):
            body(i)
            return carry

        lax.fori_loop(lo, hi, step, 0)

    return run


def kernel(
    n, slot_ref, ids_ref, prob_ref, tok_ref, wg_hbm, wu_hbm, wd_hbm, out_ref,
    wg, wu, wd, own, raw, x, gacc, uacc, hid, part, rin, lin, rout, lout,
    wsem, raw_s, raw_r, x_s, x_r, r_s, r_r, l_s, l_r,
):
    me = lax.axis_index("expert")
    chunks, cap, width = own.shape
    pairs = n // 2
    hidden = hid.shape[1]
    tile = min(512, hidden)
    pair = me // 2
    odd = me % 2
    partner = me + 1 - 2 * odd
    has_left, has_right = me > 0, me < n - 1

    def weight(which, k):
        rows = pl.ds(pl.multiple_of(k * width, width), width)
        if which == 0:
            return pltpu.make_async_copy(wg_hbm.at[rows, :], wg.at[k], wsem.at[0, k])
        if which == 1:
            return pltpu.make_async_copy(wu_hbm.at[rows, :], wu.at[k], wsem.at[1, k])
        return pltpu.make_async_copy(wd_hbm.at[:, rows], wd.at[k], wsem.at[2, k])

    def remote(src, dst, ssem, rsem, to):
        return pltpu.make_async_remote_copy(
            src_ref=src, dst_ref=dst, send_sem=ssem, recv_sem=rsem,
            device_id={"expert": to}, device_id_type=MESH,
        )

    def raw_copy(k):
        return remote(own.at[k], raw.at[k], raw_s.at[k], raw_r.at[k], partner)

    def x_copy(q, k, to):
        return remote(x.at[q, k], x.at[q, k], x_s.at[q, k], x_r.at[q, k], to)

    def r_copy(q, j):
        return remote(rout.at[q, j], rin.at[q, j], r_s.at[q, j], r_r.at[q, j], me + 1)

    def l_copy(q, j):
        return remote(lout.at[q, j], lin.at[q, j], l_s.at[q, j], l_r.at[q, j], me - 1)

    barrier = pltpu.get_barrier_semaphore()

    @pl.when(has_left)
    def _():
        pl.semaphore_signal(barrier, inc=1, device_id={"expert": me - 1}, device_id_type=MESH)

    @pl.when(has_right)
    def _():
        pl.semaphore_signal(barrier, inc=1, device_id={"expert": me + 1}, device_id_type=MESH)

    @loop(0, chunks)
    def _(k):
        weight(0, k).start()
        weight(1, k).start()

    @loop(0, chunks)
    def _(k):
        weight(2, k).start()

    slot = slot_ref[...]
    routed = slot < cap
    count = jnp.sum(routed.astype(jnp.int32), axis=1, keepdims=True)
    row = slot + odd * (cap - count)
    at = lax.broadcasted_iota(jnp.int32, (cap, slot.shape[1]), 0)
    pick = (at == row) & routed
    pick_half = jnp.where(pick, 1.0, 0.0).astype(BF16)
    prob = prob_ref[...]
    share = jnp.where(ids_ref[0:1, :] == 0, prob, jnp.where(ids_ref[1:2, :] == 0, 1.0 - prob, 0.0))
    row_share = jnp.sum(jnp.where(pick, share, 0.0), axis=1, keepdims=True)

    pl.semaphore_wait(barrier, has_left.astype(jnp.int32) + has_right.astype(jnp.int32))

    for k in range(chunks):
        own[k] = jnp.dot(
            pick_half, tok_ref[:, k * width:(k + 1) * width], preferred_element_type=F32
        ).astype(BF16)
        raw_copy(k).start()

    def forwards(q):
        return ((q < pair) & has_right) | ((q > pair) & has_left)

    def forward(k):
        for q in range(pairs):
            @pl.when(forwards(q))
            def _():
                to = jnp.where(q < pair, me + 1, me - 1)
                x_copy(q, k, to).wait_recv()
                x_copy(q, k, to).start()

    def project(q, k):
        block = x[q, k]
        for t in range(0, hidden, tile):
            cols = slice(t, t + tile)
            gate = jnp.dot(block, wg[k, :, cols], preferred_element_type=F32)
            up = jnp.dot(block, wu[k, :, cols], preferred_element_type=F32)
            gacc[:, cols] += gate
            uacc[:, cols] += up

    def finish(q, first):
        for t in range(0, hidden, tile):
            cols = slice(t, t + tile)
            gate = gacc[:, cols]
            hid[:, cols] = (gate / (1.0 + jnp.exp(-gate)) * uacc[:, cols]).astype(BF16)

        @loop(0, chunks)
        def _(j):
            if first:
                weight(2, j).wait()
            value = jnp.dot(hid[...], wd[j], preferred_element_type=F32)
            part[q, j] = value

            @pl.when(me == 0)
            def _():
                rout[q, j] = value.astype(BF16)
                r_copy(q, j).start()

            @pl.when(me == n - 1)
            def _():
                lout[q, j] = value.astype(BF16)
                l_copy(q, j).start()

    gacc[...] = jnp.zeros_like(gacc)
    uacc[...] = jnp.zeros_like(uacc)

    @loop(0, chunks)
    def _(k):
        raw_copy(k).wait_recv()
        x[pair, k] = own[k] + raw[k]

        @pl.when((odd == 1) & has_right)
        def _():
            x_copy(pair, k, me + 1).start()

        @pl.when((odd == 0) & has_left)
        def _():
            x_copy(pair, k, me - 1).start()

        @pl.when(k > 0)
        def _():
            forward(k - 1)

        weight(0, k).wait()
        weight(1, k).wait()
        project(pair, k)

    forward(chunks - 1)
    finish(pair, True)

    @loop(1, pairs)
    def _(s):
        q = lax.rem(pair + s, pairs)
        gacc[...] = jnp.zeros_like(gacc)
        uacc[...] = jnp.zeros_like(uacc)

        @loop(0, chunks)
        def _(k):
            @pl.when(jnp.logical_not(forwards(q)))
            def _():
                x_copy(q, k, partner).wait_recv()

            project(q, k)

        finish(q, False)

    @loop(0, chunks)
    def _(j):
        for q in range(pairs):
            @pl.when(has_left & (me <= 2 * q))
            def _():
                r_copy(q, j).wait_recv()
                value = part[q, j] + rin[q, j].astype(F32)
                part[q, j] = value
                rout[q, j] = value.astype(BF16)
                r_copy(q, j).start()

            @pl.when(has_right & (me >= 2 * q + 1))
            def _():
                l_copy(q, j).wait_recv()
                value = part[q, j] + lin[q, j].astype(F32)
                part[q, j] = value
                lout[q, j] = value.astype(BF16)
                l_copy(q, j).start()

        def place(down):
            scaled = (row_share * down).astype(BF16)
            cols = pl.ds(pl.multiple_of(j * width, width), width)
            out_ref[:, cols] = lax.dot_general(
                pick_half, scaled, (((0,), (0,)), ((), ())), preferred_element_type=F32
            ).astype(BF16)

        @pl.when(odd == 0)
        def _():
            l_copy(pair, j).wait_recv()
            place(part[pair, j] + lin[pair, j].astype(F32))

        @pl.when(odd == 1)
        def _():
            r_copy(pair, j).wait_recv()
            place(part[pair, j] + rin[pair, j].astype(F32))

    @loop(0, chunks)
    def _(k):
        raw_copy(k).wait_send()

        @pl.when(((odd == 1) & has_right) | ((odd == 0) & has_left))
        def _():
            x_copy(pair, k, partner).wait_send()

        for q in range(pairs):
            @pl.when(forwards(q))
            def _():
                x_copy(q, k, partner).wait_send()

            @pl.when(me <= 2 * q)
            def _():
                r_copy(q, k).wait_send()

            @pl.when(me >= 2 * q + 1)
            def _():
                l_copy(q, k).wait_send()


def shards(n, tokens, w_gate, w_up, w_down, route_ids, route_prob, slot_index):
    count, model = tokens.shape
    hidden = w_gate.shape[1]
    cap = count // 2
    pairs = n // 2
    width = 512
    chunks = model // width
    flow = pltpu.VMEM((pairs, chunks, cap, width), BF16)
    dma = pltpu.SemaphoreType.DMA
    vmem = pl.BlockSpec(memory_space=pltpu.VMEM)
    hbm = pl.BlockSpec(memory_space=pl.ANY)
    return pl.pallas_call(
        functools.partial(kernel, n),
        out_shape=jax.ShapeDtypeStruct((count, model), BF16),
        in_specs=[vmem] * 4 + [hbm] * 3,
        out_specs=vmem,
        scratch_shapes=[
            pltpu.VMEM((chunks, width, hidden), BF16),
            pltpu.VMEM((chunks, width, hidden), BF16),
            pltpu.VMEM((chunks, hidden, width), BF16),
            pltpu.VMEM((chunks, cap, width), BF16),
            pltpu.VMEM((chunks, cap, width), BF16),
            flow,
            pltpu.VMEM((cap, hidden), F32),
            pltpu.VMEM((cap, hidden), F32),
            pltpu.VMEM((cap, hidden), BF16),
            pltpu.VMEM((pairs, chunks, cap, width), F32),
            flow, flow, flow, flow,
            dma((3, chunks)),
            dma((chunks,)), dma((chunks,)),
            dma((pairs, chunks)), dma((pairs, chunks)),
            dma((pairs, chunks)), dma((pairs, chunks)),
            dma((pairs, chunks)), dma((pairs, chunks)),
        ],
        compiler_params=pltpu.CompilerParams(
            collective_id=0, has_side_effects=True, vmem_limit_bytes=60 * 2**20
        ),
        cost_estimate=pl.CostEstimate(
            flops=6 * pairs * cap * model * hidden,
            bytes_accessed=6 * model * hidden,
            transcendentals=pairs * cap * hidden,
        ),
    )(slot_index[None, :], route_ids.T, route_prob[None, :], tokens, w_gate, w_up, w_down)


def solution(mesh):
    return jax.shard_map(
        functools.partial(shards, mesh.shape["expert"]),
        mesh=mesh,
        in_specs=(
            P(("dp", "expert"), None),
            P(None, "expert"),
            P(None, "expert"),
            P("expert", None),
            P(("dp", "expert"), None),
            P(("dp", "expert")),
            P(("dp", "expert")),
        ),
        out_specs=P(("dp", "expert"), None),
        check_vma=False,
    )
```

time: 120 us -> 79.9 us (0.67)
  Pallas kernels: 0 us -> 77.5 us
  waiting for transfers between devices: 74.1 us -> 0 us
  matrix products: 30.9 us -> 0 us
  between operations: 13.4 us -> 0.01 us
    pallas_call x0 -> x1, Pallas kernels: none -> 77.5 us  [shards(): pl.pallas_call(functools.partial(kernel, n), out_shape=jax.ShapeDtypeStru...]
    all_gather x1 -> x0, waiting for transfers between devices: 39.9 us -> none  [shards(): block = lax.all_gather(source, 'expert', axis=0, tiled=True)]
    reduce_scatter x1 -> x0, waiting for transfers between devices: 34.1 us -> none  [shards(): lax.psum_scatter(terms.astype(jnp.bfloat16), 'expert', scatter_dimension=...]
    dot_general x5 -> x0, matrix products: 30.9 us -> none  [the longest x1 16.9 us: shards(): jnp.dot(hidden, w_down, preferred_element_type=jnp.float32)]
  transfers between devices with their start and end apart: 2 -> 0, of which waited for: 2 -> 0; matrix products, arithmetic and copies ran while one was open for 0% -> 0% of each run, Pallas kernels for 0% -> 0%
where the time goes in v1:
time: 79.9 us; the launch traced here: 79.6 us
  Pallas kernels  77.5 us (97%)
  local copies, waits for them, and re-layouts  2.06 us (3%)
    pallas_call x1, Pallas kernels, shards(): pl.pallas_call(functools.partial(kernel, n), out_shape=jax.ShapeDtypeStru...  77.5 us
    unnamed x1, local copies, waits for them, and re-layouts  2.06 us

profile of v1, /device:TPU:0, one launch (start us, length us, event | category | flops | bytes accessed | tf_op | source)
XLA Modules:
  0.0 79.6 jit_solution(7055957675746463125)
XLA Ops:
  0.0 77.5 %shard_map.73 = bf16[128,3072]{1,0:T(8,128)(2,1)} custom-call(s32[1,128]{1,0:T(1,128)} %bitcast.4, s32[2,128]{1,0:T(2,128)} %bitcast.3, f32[1,128]{1,0:T(1,128)} %bitcast.5, bf16[128,3072]{1,0:T(8,128)(2,1)} %tok_ref.1, bf16[3072,2048]{1,0:T(8,128)(2,1)} %wg_hbm.1, bf16[3072,2048]{1,0:T(8,128)(2,1)} %wu_hbm.1, bf16[2048,3072]{1,0:T(8,128)(2,1)} %wd_hbm.1), custom_call_target="tpu_custom_call" | custom-call | flops 4831838208 | bytes 37748736 | tf_op jit(solution)/shard_map/pallas_call | solution.py:260
  77.5 2.1 %copy.9 = bf16[128,3072]{1,0:T(8,128)(2,1)} copy(bf16[128,3072]{1,0:T(8,128)(2,1)} %shard_map.73) | data formatting | bytes 1572864

commit v2 on v1

--- a/solution.py
+++ b/solution.py
@@ -33,6 +33,7 @@
     pairs = n // 2
     hidden = hid.shape[1]
     tile = min(512, hidden)
+    ahead = min(2, chunks)
     pair = me // 2
     odd = me % 2
     partner = me + 1 - 2 * odd
@@ -55,8 +56,12 @@
     def raw_copy(k):
         return remote(own.at[k], raw.at[k], raw_s.at[k], raw_r.at[k], partner)
 
+    def rows_of(q):
+        return pl.ds(pl.multiple_of(q * cap, cap), cap)
+
     def x_copy(q, k, to):
-        return remote(x.at[q, k], x.at[q, k], x_s.at[q, k], x_r.at[q, k], to)
+        block = x.at[k, rows_of(q), :]
+        return remote(block, block, x_s.at[q, k], x_r.at[q, k], to)
 
     def r_copy(q, j):
         return remote(rout.at[q, j], rin.at[q, j], r_s.at[q, j], r_r.at[q, j], me + 1)
@@ -100,50 +105,30 @@
         own[k] = jnp.dot(
             pick_half, tok_ref[:, k * width:(k + 1) * width], preferred_element_type=F32
         ).astype(BF16)
-        raw_copy(k).start()
+        if k < ahead:
+            raw_copy(k).start()
 
     def forwards(q):
         return ((q < pair) & has_right) | ((q > pair) & has_left)
 
-    def forward(k):
+    def project(k):
         for q in range(pairs):
-            @pl.when(forwards(q))
+            @pl.when(q != pair)
             def _():
                 to = jnp.where(q < pair, me + 1, me - 1)
                 x_copy(q, k, to).wait_recv()
-                x_copy(q, k, to).start()
-
-    def project(q, k):
-        block = x[q, k]
+
+                @pl.when(forwards(q))
+                def _():
+                    x_copy(q, k, to).start()
+
+        weight(0, k).wait()
+        weight(1, k).wait()
+        block = x[k]
         for t in range(0, hidden, tile):
             cols = slice(t, t + tile)
-            gate = jnp.dot(block, wg[k, :, cols], preferred_element_type=F32)
-            up = jnp.dot(block, wu[k, :, cols], preferred_element_type=F32)
-            gacc[:, cols] += gate
-            uacc[:, cols] += up
-
-    def finish(q, first):
-        for t in range(0, hidden, tile):
-            cols = slice(t, t + tile)
-            gate = gacc[:, cols]
-            hid[:, cols] = (gate / (1.0 + jnp.exp(-gate)) * uacc[:, cols]).astype(BF16)
-
-        @loop(0, chunks)
-        def _(j):
-            if first:
-                weight(2, j).wait()
-            value = jnp.dot(hid[...], wd[j], preferred_element_type=F32)
-            part[q, j] = value
-
-            @pl.when(me == 0)
-            def _():
-                rout[q, j] = value.astype(BF16)
-                r_copy(q, j).start()
-
-            @pl.when(me == n - 1)
-            def _():
-                lout[q, j] = value.astype(BF16)
-                l_copy(q, j).start()
+            gacc[:, cols] += jnp.dot(block, wg[k, :, cols], preferred_element_type=F32)
+            uacc[:, cols] += jnp.dot(block, wu[k, :, cols], preferred_element_type=F32)
 
     gacc[...] = jnp.zeros_like(gacc)
     uacc[...] = jnp.zeros_like(uacc)
@@ -151,7 +136,7 @@
     @loop(0, chunks)
     def _(k):
         raw_copy(k).wait_recv()
-        x[pair, k] = own[k] + raw[k]
+        x[k, rows_of(pair), :] = own[k] + raw[k]
 
         @pl.when((odd == 1) & has_right)
         def _():
@@ -161,32 +146,44 @@
         def _():
             x_copy(pair, k, me - 1).start()
 
+        @pl.when(k + ahead < chunks)
+        def _():
+            raw_copy(k + ahead).start()
+
         @pl.when(k > 0)
         def _():
-            forward(k - 1)
-
-        weight(0, k).wait()
-        weight(1, k).wait()
-        project(pair, k)
-
-    forward(chunks - 1)
-    finish(pair, True)
-
-    @loop(1, pairs)
-    def _(s):
-        q = lax.rem(pair + s, pairs)
-        gacc[...] = jnp.zeros_like(gacc)
-        uacc[...] = jnp.zeros_like(uacc)
-
-        @loop(0, chunks)
-        def _(k):
-            @pl.when(jnp.logical_not(forwards(q)))
-            def _():
-                x_copy(q, k, partner).wait_recv()
-
-            project(q, k)
-
-        finish(q, False)
+            project(k - 1)
+
+    project(chunks - 1)
+
+    for t in range(0, hidden, tile):
+        cols = slice(t, t + tile)
+        gate = gacc[:, cols]
+        hid[:, cols] = (gate / (1.0 + jnp.exp(-gate)) * uacc[:, cols]).astype(BF16)
+
+    def send_from_ends(q, j):
+        @pl.when(me == 0)
+        def _():
+            rout[q, j] = part[j, rows_of(q), :].astype(BF16)
+            r_copy(q, j).start()
+
+        @pl.when(me == n - 1)
+        def _():
+            lout[q, j] = part[j, rows_of(q), :].astype(BF16)
+            l_copy(q, j).start()
+
+    @loop(0, chunks)
+    def _(j):
+        weight(2, j).wait()
+        part[j] = jnp.dot(hid[...], wd[j], preferred_element_type=F32)
+        for q in range(pairs):
+            @pl.when(q != pair)
+            def _():
+                send_from_ends(q, j)
+
+    @loop(0, chunks)
+    def _(j):
+        send_from_ends(pair, j)
 
     @loop(0, chunks)
     def _(j):
@@ -194,20 +191,23 @@
             @pl.when(has_left & (me <= 2 * q))
             def _():
                 r_copy(q, j).wait_recv()
-                value = part[q, j] + rin[q, j].astype(F32)
-                part[q, j] = value
+                value = part[j, rows_of(q), :] + rin[q, j].astype(F32)
+                part[j, rows_of(q), :] = value
                 rout[q, j] = value.astype(BF16)
                 r_copy(q, j).start()
 
             @pl.when(has_right & (me >= 2 * q + 1))
             def _():
                 l_copy(q, j).wait_recv()
-                value = part[q, j] + lin[q, j].astype(F32)
-                part[q, j] = value
+                value = part[j, rows_of(q), :] + lin[q, j].astype(F32)
+                part[j, rows_of(q), :] = value
                 lout[q, j] = value.astype(BF16)
                 l_copy(q, j).start()
 
-        def place(down):
+    @loop(0, chunks)
+    def _(j):
+        def place(other):
+            down = part[j, rows_of(pair), :] + other.astype(F32)
             scaled = (row_share * down).astype(BF16)
             cols = pl.ds(pl.multiple_of(j * width, width), width)
             out_ref[:, cols] = lax.dot_general(
@@ -217,12 +217,12 @@
         @pl.when(odd == 0)
         def _():
             l_copy(pair, j).wait_recv()
-            place(part[pair, j] + lin[pair, j].astype(F32))
+            place(lin[pair, j])
 
         @pl.when(odd == 1)
         def _():
             r_copy(pair, j).wait_recv()
-            place(part[pair, j] + rin[pair, j].astype(F32))
+            place(rin[pair, j])
 
     @loop(0, chunks)
     def _(k):
@@ -251,6 +251,7 @@
     hidden = w_gate.shape[1]
     cap = count // 2
     pairs = n // 2
+    rows = pairs * cap
     width = 512
     chunks = model // width
     flow = pltpu.VMEM((pairs, chunks, cap, width), BF16)
@@ -268,11 +269,11 @@
             pltpu.VMEM((chunks, hidden, width), BF16),
             pltpu.VMEM((chunks, cap, width), BF16),
             pltpu.VMEM((chunks, cap, width), BF16),
-            flow,
-            pltpu.VMEM((cap, hidden), F32),
-            pltpu.VMEM((cap, hidden), F32),
-            pltpu.VMEM((cap, hidden), BF16),
-            pltpu.VMEM((pairs, chunks, cap, width), F32),
+            pltpu.VMEM((chunks, rows, width), BF16),
+            pltpu.VMEM((rows, hidden), F32),
+            pltpu.VMEM((rows, hidden), F32),
+            pltpu.VMEM((rows, hidden), BF16),
+            pltpu.VMEM((chunks, rows, width), F32),
             flow, flow, flow, flow,
             dma((3, chunks)),
             dma((chunks,)), dma((chunks,)),

time: 79.9 us -> 78.2 us (0.979)
  Pallas kernels: 77.5 us -> 75.7 us
    pallas_call x1, Pallas kernels: 77.5 us -> 75.7 us  [shards(): pl.pallas_call(functools.partial(kernel, n), out_shape=jax.ShapeDtypeStru...]
where the time goes in v2:
time: 78.2 us; the launch traced here: 77.8 us
  Pallas kernels  75.7 us (97%)
  local copies, waits for them, and re-layouts  2.06 us (3%)
    pallas_call x1, Pallas kernels, shards(): pl.pallas_call(functools.partial(kernel, n), out_shape=jax.ShapeDtypeStru...  75.7 us
    unnamed x1, local copies, waits for them, and re-layouts  2.06 us

profile of v2, /device:TPU:0, one launch (start us, length us, event | category | flops | bytes accessed | tf_op | source)
XLA Modules:
  0.0 77.8 jit_solution(11505239631850520438)
XLA Ops:
  0.0 75.7 %shard_map.73 = bf16[128,3072]{1,0:T(8,128)(2,1)} custom-call(s32[1,128]{1,0:T(1,128)} %bitcast.4, s32[2,128]{1,0:T(2,128)} %bitcast.3, f32[1,128]{1,0:T(1,128)} %bitcast.5, bf16[128,3072]{1,0:T(8,128)(2,1)} %tok_ref.1, bf16[3072,2048]{1,0:T(8,128)(2,1)} %wg_hbm.1, bf16[3072,2048]{1,0:T(8,128)(2,1)} %wu_hbm.1, bf16[2048,3072]{1,0:T(8,128)(2,1)} %wd_hbm.1), custom_call_target="tpu_custom_call" | custom-call | flops 4831838208 | bytes 37748736 | tf_op jit(solution)/shard_map/pallas_call | solution.py:261
  75.7 2.1 %copy.9 = bf16[128,3072]{1,0:T(8,128)(2,1)} copy(bf16[128,3072]{1,0:T(8,128)(2,1)} %shard_map.73) | data formatting | bytes 1572864

commit v3 on v2

--- a/solution.py
+++ b/solution.py
@@ -34,6 +34,7 @@
     hidden = hid.shape[1]
     tile = min(512, hidden)
     ahead = min(2, chunks)
+    window = min(3, chunks)
     pair = me // 2
     odd = me % 2
     partner = me + 1 - 2 * odd
@@ -78,15 +79,6 @@
     @pl.when(has_right)
     def _():
         pl.semaphore_signal(barrier, inc=1, device_id={"expert": me + 1}, device_id_type=MESH)
-
-    @loop(0, chunks)
-    def _(k):
-        weight(0, k).start()
-        weight(1, k).start()
-
-    @loop(0, chunks)
-    def _(k):
-        weight(2, k).start()
 
     slot = slot_ref[...]
     routed = slot < cap
@@ -108,6 +100,10 @@
         if k < ahead:
             raw_copy(k).start()
 
+    for k in range(window):
+        weight(0, k).start()
+        weight(1, k).start()
+
     def forwards(q):
         return ((q < pair) & has_right) | ((q > pair) & has_left)
 
@@ -124,6 +120,16 @@
 
         weight(0, k).wait()
         weight(1, k).wait()
+
+        @pl.when(k + window < chunks)
+        def _():
+            weight(0, k + window).start()
+            weight(1, k + window).start()
+
+        @pl.when(k + window >= chunks)
+        def _():
+            weight(2, k + window - chunks).start()
+
         block = x[k]
         for t in range(0, hidden, tile):
             cols = slice(t, t + tile)
@@ -154,7 +160,7 @@
         def _():
             project(k - 1)
 
-    project(chunks - 1)
+    project(jnp.int32(chunks - 1))
 
     for t in range(0, hidden, tile):
         cols = slice(t, t + tile)
@@ -175,6 +181,11 @@
     @loop(0, chunks)
     def _(j):
         weight(2, j).wait()
+
+        @pl.when(j + window < chunks)
+        def _():
+            weight(2, j + window).start()
+
         part[j] = jnp.dot(hid[...], wd[j], preferred_element_type=F32)
         for q in range(pairs):
             @pl.when(q != pair)

time: 78.2 us -> 78.2 us (level)
  no operation moved by 1% of the time
where the time goes in v3:
time: 78.2 us; the launch traced here: 77.9 us
  Pallas kernels  75.8 us (97%)
  local copies, waits for them, and re-layouts  2.06 us (3%)
    pallas_call x1, Pallas kernels, shards(): pl.pallas_call(functools.partial(kernel, n), out_shape=jax.ShapeDtypeStru...  75.8 us
    unnamed x1, local copies, waits for them, and re-layouts  2.06 us

profile of v3, /device:TPU:0, one launch (start us, length us, event | category | flops | bytes accessed | tf_op | source)
XLA Modules:
  0.0 77.9 jit_solution(3512169597807292544)
XLA Ops:
  0.0 75.8 %shard_map.73 = bf16[128,3072]{1,0:T(8,128)(2,1)} custom-call(s32[1,128]{1,0:T(1,128)} %bitcast.4, s32[2,128]{1,0:T(2,128)} %bitcast.3, f32[1,128]{1,0:T(1,128)} %bitcast.5, bf16[128,3072]{1,0:T(8,128)(2,1)} %tok_ref.1, bf16[3072,2048]{1,0:T(8,128)(2,1)} %wg_hbm.1, bf16[3072,2048]{1,0:T(8,128)(2,1)} %wu_hbm.1, bf16[2048,3072]{1,0:T(8,128)(2,1)} %wd_hbm.1), custom_call_target="tpu_custom_call" | custom-call | flops 4831838208 | bytes 37748736 | tf_op jit(solution)/shard_map/pallas_call | solution.py:272
  75.8 2.1 %copy.9 = bf16[128,3072]{1,0:T(8,128)(2,1)} copy(bf16[128,3072]{1,0:T(8,128)(2,1)} %shard_map.73) | data formatting | bytes 1572864

commit v4 on v2

--- a/solution.py
+++ b/solution.py
@@ -33,7 +33,6 @@
     pairs = n // 2
     hidden = hid.shape[1]
     tile = min(512, hidden)
-    ahead = min(2, chunks)
     pair = me // 2
     odd = me % 2
     partner = me + 1 - 2 * odd
@@ -78,15 +77,6 @@
     @pl.when(has_right)
     def _():
         pl.semaphore_signal(barrier, inc=1, device_id={"expert": me + 1}, device_id_type=MESH)
-
-    @loop(0, chunks)
-    def _(k):
-        weight(0, k).start()
-        weight(1, k).start()
-
-    @loop(0, chunks)
-    def _(k):
-        weight(2, k).start()
 
     slot = slot_ref[...]
     routed = slot < cap
@@ -105,22 +95,55 @@
         own[k] = jnp.dot(
             pick_half, tok_ref[:, k * width:(k + 1) * width], preferred_element_type=F32
         ).astype(BF16)
-        if k < ahead:
-            raw_copy(k).start()
+        raw_copy(k).start()
+
+    @loop(0, chunks)
+    def _(k):
+        weight(0, k).start()
+        weight(1, k).start()
+
+    @loop(0, chunks)
+    def _(k):
+        weight(2, k).start()
 
     def forwards(q):
         return ((q < pair) & has_right) | ((q > pair) & has_left)
 
-    def project(k):
-        for q in range(pairs):
-            @pl.when(q != pair)
-            def _():
-                to = jnp.where(q < pair, me + 1, me - 1)
-                x_copy(q, k, to).wait_recv()
-
-                @pl.when(forwards(q))
-                def _():
-                    x_copy(q, k, to).start()
+    def forward(k):
+        for q in range(pairs):
+            @pl.when(forwards(q))
+            def _():
+                x_copy(q, k, partner).wait_recv()
+                x_copy(q, k, jnp.where(q < pair, me + 1, me - 1)).start()
+
+    @loop(0, chunks)
+    def _(k):
+        raw_copy(k).wait_recv()
+        x[k, rows_of(pair), :] = own[k] + raw[k]
+
+        @pl.when((odd == 1) & has_right)
+        def _():
+            x_copy(pair, k, me + 1).start()
+
+        @pl.when((odd == 0) & has_left)
+        def _():
+            x_copy(pair, k, me - 1).start()
+
+        @pl.when(k > 0)
+        def _():
+            forward(k - 1)
+
+    forward(chunks - 1)
+
+    gacc[...] = jnp.zeros_like(gacc)
+    uacc[...] = jnp.zeros_like(uacc)
+
+    @loop(0, chunks)
+    def _(k):
+        for q in range(pairs):
+            @pl.when((q != pair) & jnp.logical_not(forwards(q)))
+            def _():
+                x_copy(q, k, partner).wait_recv()
 
         weight(0, k).wait()
         weight(1, k).wait()
@@ -129,32 +152,6 @@
             cols = slice(t, t + tile)
             gacc[:, cols] += jnp.dot(block, wg[k, :, cols], preferred_element_type=F32)
             uacc[:, cols] += jnp.dot(block, wu[k, :, cols], preferred_element_type=F32)
-
-    gacc[...] = jnp.zeros_like(gacc)
-    uacc[...] = jnp.zeros_like(uacc)
-
-    @loop(0, chunks)
-    def _(k):
-        raw_copy(k).wait_recv()
-        x[k, rows_of(pair), :] = own[k] + raw[k]
-
-        @pl.when((odd == 1) & has_right)
-        def _():
-            x_copy(pair, k, me + 1).start()
-
-        @pl.when((odd == 0) & has_left)
-        def _():
-            x_copy(pair, k, me - 1).start()
-
-        @pl.when(k + ahead < chunks)
-        def _():
-            raw_copy(k + ahead).start()
-
-        @pl.when(k > 0)
-        def _():
-            project(k - 1)
-
-    project(chunks - 1)
 
     for t in range(0, hidden, tile):
         cols = slice(t, t + tile)

time: 78.2 us -> 73.9 us (0.945)
  Pallas kernels: 75.7 us -> 71.5 us
    pallas_call x1, Pallas kernels: 75.7 us -> 71.5 us  [shards(): pl.pallas_call(functools.partial(kernel, n), out_shape=jax.ShapeDtypeStru...]
where the time goes in v4:
time: 73.9 us; the launch traced here: 73.5 us
  Pallas kernels  71.5 us (97%)
  local copies, waits for them, and re-layouts  2.06 us (3%)
    pallas_call x1, Pallas kernels, shards(): pl.pallas_call(functools.partial(kernel, n), out_shape=jax.ShapeDtypeStru...  71.5 us
    unnamed x1, local copies, waits for them, and re-layouts  2.06 us

profile of v4, /device:TPU:0, one launch (start us, length us, event | category | flops | bytes accessed | tf_op | source)
XLA Modules:
  0.0 73.5 jit_solution(17191856817565143002)
XLA Ops:
  0.0 71.5 %shard_map.73 = bf16[128,3072]{1,0:T(8,128)(2,1)} custom-call(s32[1,128]{1,0:T(1,128)} %bitcast.4, s32[2,128]{1,0:T(2,128)} %bitcast.3, f32[1,128]{1,0:T(1,128)} %bitcast.5, bf16[128,3072]{1,0:T(8,128)(2,1)} %tok_ref.1, bf16[3072,2048]{1,0:T(8,128)(2,1)} %wg_hbm.1, bf16[3072,2048]{1,0:T(8,128)(2,1)} %wu_hbm.1, bf16[2048,3072]{1,0:T(8,128)(2,1)} %wd_hbm.1), custom_call_target="tpu_custom_call" | custom-call | flops 4831838208 | bytes 37748736 | tf_op jit(solution)/shard_map/pallas_call | solution.py:258
  71.5 2.1 %copy.9 = bf16[128,3072]{1,0:T(8,128)(2,1)} copy(bf16[128,3072]{1,0:T(8,128)(2,1)} %shard_map.73) | data formatting | bytes 1572864

commit v5 on v4

--- a/solution.py
+++ b/solution.py
@@ -135,52 +135,53 @@
 
     forward(chunks - 1)
 
-    gacc[...] = jnp.zeros_like(gacc)
-    uacc[...] = jnp.zeros_like(uacc)
-
-    @loop(0, chunks)
-    def _(k):
-        for q in range(pairs):
-            @pl.when((q != pair) & jnp.logical_not(forwards(q)))
+    def send_from_ends(q, j):
+        @pl.when(me == 0)
+        def _():
+            rout[q, j] = part[j, rows_of(q), :].astype(BF16)
+            r_copy(q, j).start()
+
+        @pl.when(me == n - 1)
+        def _():
+            lout[q, j] = part[j, rows_of(q), :].astype(BF16)
+            l_copy(q, j).start()
+
+    @loop(0, pairs)
+    def _(step):
+        q = lax.rem(pair + step, pairs)
+        gacc[...] = jnp.zeros_like(gacc)
+        uacc[...] = jnp.zeros_like(uacc)
+
+        @loop(0, chunks)
+        def _(k):
+            @pl.when((step > 0) & jnp.logical_not(forwards(q)))
             def _():
                 x_copy(q, k, partner).wait_recv()
 
-        weight(0, k).wait()
-        weight(1, k).wait()
-        block = x[k]
+            @pl.when(step == 0)
+            def _():
+                weight(0, k).wait()
+                weight(1, k).wait()
+
+            block = x[k, rows_of(q), :]
+            for t in range(0, hidden, tile):
+                cols = slice(t, t + tile)
+                gacc[:, cols] += jnp.dot(block, wg[k, :, cols], preferred_element_type=F32)
+                uacc[:, cols] += jnp.dot(block, wu[k, :, cols], preferred_element_type=F32)
+
         for t in range(0, hidden, tile):
             cols = slice(t, t + tile)
-            gacc[:, cols] += jnp.dot(block, wg[k, :, cols], preferred_element_type=F32)
-            uacc[:, cols] += jnp.dot(block, wu[k, :, cols], preferred_element_type=F32)
-
-    for t in range(0, hidden, tile):
-        cols = slice(t, t + tile)
-        gate = gacc[:, cols]
-        hid[:, cols] = (gate / (1.0 + jnp.exp(-gate)) * uacc[:, cols]).astype(BF16)
-
-    def send_from_ends(q, j):
-        @pl.when(me == 0)
-        def _():
-            rout[q, j] = part[j, rows_of(q), :].astype(BF16)
-            r_copy(q, j).start()
-
-        @pl.when(me == n - 1)
-        def _():
-            lout[q, j] = part[j, rows_of(q), :].astype(BF16)
-            l_copy(q, j).start()
-
-    @loop(0, chunks)
-    def _(j):
-        weight(2, j).wait()
-        part[j] = jnp.dot(hid[...], wd[j], preferred_element_type=F32)
-        for q in range(pairs):
-            @pl.when(q != pair)
-            def _():
-                send_from_ends(q, j)
-
-    @loop(0, chunks)
-    def _(j):
-        send_from_ends(pair, j)
+            gate = gacc[:, cols]
+            hid[:, cols] = (gate / (1.0 + jnp.exp(-gate)) * uacc[:, cols]).astype(BF16)
+
+        @loop(0, chunks)
+        def _(j):
+            @pl.when(step == 0)
+            def _():
+                weight(2, j).wait()
+
+            part[j, rows_of(q), :] = jnp.dot(hid[...], wd[j], preferred_element_type=F32)
+            send_from_ends(q, j)
 
     @loop(0, chunks)
     def _(j):
@@ -267,9 +268,9 @@
             pltpu.VMEM((chunks, cap, width), BF16),
             pltpu.VMEM((chunks, cap, width), BF16),
             pltpu.VMEM((chunks, rows, width), BF16),
-            pltpu.VMEM((rows, hidden), F32),
-            pltpu.VMEM((rows, hidden), F32),
-            pltpu.VMEM((rows, hidden), BF16),
+            pltpu.VMEM((cap, hidden), F32),
+            pltpu.VMEM((cap, hidden), F32),
+            pltpu.VMEM((cap, hidden), BF16),
             pltpu.VMEM((chunks, rows, width), F32),
             flow, flow, flow, flow,
             dma((3, chunks)),

time: 73.9 us -> 81.6 us (1.10)
  Pallas kernels: 71.5 us -> 79.2 us
    pallas_call x1, Pallas kernels: 71.5 us -> 79.2 us  [shards(): pl.pallas_call(functools.partial(kernel, n), out_shape=jax.ShapeDtypeStru...]
where the time goes in v5:
time: 81.6 us; the launch traced here: 81.3 us
  Pallas kernels  79.2 us (97%)
  local copies, waits for them, and re-layouts  2.06 us (3%)
    pallas_call x1, Pallas kernels, shards(): pl.pallas_call(functools.partial(kernel, n), out_shape=jax.ShapeDtypeStru...  79.2 us
    unnamed x1, local copies, waits for them, and re-layouts  2.06 us

profile of v5, /device:TPU:0, one launch (start us, length us, event | category | flops | bytes accessed | tf_op | source)
XLA Modules:
  0.0 81.3 jit_solution(17245922060542621048)
XLA Ops:
  0.0 79.2 %shard_map.73 = bf16[128,3072]{1,0:T(8,128)(2,1)} custom-call(s32[1,128]{1,0:T(1,128)} %bitcast.4, s32[2,128]{1,0:T(2,128)} %bitcast.3, f32[1,128]{1,0:T(1,128)} %bitcast.5, bf16[128,3072]{1,0:T(8,128)(2,1)} %tok_ref.1, bf16[3072,2048]{1,0:T(8,128)(2,1)} %wg_hbm.1, bf16[3072,2048]{1,0:T(8,128)(2,1)} %wu_hbm.1, bf16[2048,3072]{1,0:T(8,128)(2,1)} %wd_hbm.1), custom_call_target="tpu_custom_call" | custom-call | flops 4831838208 | bytes 37748736 | tf_op jit(solution)/shard_map/pallas_call | solution.py:259
  79.2 2.1 %copy.9 = bf16[128,3072]{1,0:T(8,128)(2,1)} copy(bf16[128,3072]{1,0:T(8,128)(2,1)} %shard_map.73) | data formatting | bytes 1572864

commit v6 on v4

--- a/solution.py
+++ b/solution.py
@@ -32,7 +32,8 @@
     chunks, cap, width = own.shape
     pairs = n // 2
     hidden = hid.shape[1]
-    tile = min(512, hidden)
+    tile = min(256, hidden)
+    group = 2 if chunks % 2 == 0 else 1
     pair = me // 2
     odd = me % 2
     partner = me + 1 - 2 * odd
@@ -135,23 +136,30 @@
 
     forward(chunks - 1)
 
-    gacc[...] = jnp.zeros_like(gacc)
-    uacc[...] = jnp.zeros_like(uacc)
-
-    @loop(0, chunks)
-    def _(k):
-        for q in range(pairs):
-            @pl.when((q != pair) & jnp.logical_not(forwards(q)))
-            def _():
-                x_copy(q, k, partner).wait_recv()
-
-        weight(0, k).wait()
-        weight(1, k).wait()
-        block = x[k]
+    def project(first, fresh):
+        taken = [first + i for i in range(group)]
+        for k in taken:
+            for q in range(pairs):
+                @pl.when((q != pair) & jnp.logical_not(forwards(q)))
+                def _():
+                    x_copy(q, k, partner).wait_recv()
+
+            weight(0, k).wait()
+            weight(1, k).wait()
         for t in range(0, hidden, tile):
             cols = slice(t, t + tile)
-            gacc[:, cols] += jnp.dot(block, wg[k, :, cols], preferred_element_type=F32)
-            uacc[:, cols] += jnp.dot(block, wu[k, :, cols], preferred_element_type=F32)
+            for total, w in ((gacc, wg), (uacc, wu)):
+                value = None if fresh else total[:, cols]
+                for k in taken:
+                    term = jnp.dot(x[k], w[k, :, cols], preferred_element_type=F32)
+                    value = term if value is None else value + term
+                total[:, cols] = value
+
+    project(0, True)
+
+    @loop(1, chunks // group)
+    def _(g):
+        project(g * group, False)
 
     for t in range(0, hidden, tile):
         cols = slice(t, t + tile)

time: 73.9 us -> 74.5 us (level)
  no operation moved by 1% of the time
where the time goes in v6:
time: 74.5 us; the launch traced here: 74.2 us
  Pallas kernels  72.1 us (97%)
  local copies, waits for them, and re-layouts  2.06 us (3%)
    pallas_call x1, Pallas kernels, shards(): pl.pallas_call(functools.partial(kernel, n), out_shape=jax.ShapeDtypeStru...  72.1 us
    unnamed x1, local copies, waits for them, and re-layouts  2.06 us

profile of v6, /device:TPU:0, one launch (start us, length us, event | category | flops | bytes accessed | tf_op | source)
XLA Modules:
  0.0 74.2 jit_solution(6623554644378736206)
XLA Ops:
  0.0 72.1 %shard_map.73 = bf16[128,3072]{1,0:T(8,128)(2,1)} custom-call(s32[1,128]{1,0:T(1,128)} %bitcast.4, s32[2,128]{1,0:T(2,128)} %bitcast.3, f32[1,128]{1,0:T(1,128)} %bitcast.5, bf16[128,3072]{1,0:T(8,128)(2,1)} %tok_ref.1, bf16[3072,2048]{1,0:T(8,128)(2,1)} %wg_hbm.1, bf16[3072,2048]{1,0:T(8,128)(2,1)} %wu_hbm.1, bf16[2048,3072]{1,0:T(8,128)(2,1)} %wd_hbm.1), custom_call_target="tpu_custom_call" | custom-call | flops 4831838208 | bytes 37748736 | tf_op jit(solution)/shard_map/pallas_call | solution.py:266
  72.1 2.1 %copy.9 = bf16[128,3072]{1,0:T(8,128)(2,1)} copy(bf16[128,3072]{1,0:T(8,128)(2,1)} %shard_map.73) | data formatting | bytes 1572864
